TPU v7x, 256 devices: a whole 4x4x8 slice. The times are simulated.
256 devices in a mesh: row: 16 (over z_hi, y, core), col: 16 (over z_lo, x).
Axes of the slice: x: 4, y: 4, z: 8 (z_hi: 2, z_lo: 4; z = z_hi * 4 + z_lo), core: 2. Of those that a mesh axis runs over, the one named last changes fastest.
Arguments:
- features: bfloat16 [32768, 256], P(('col', 'row')), may hold values from -6 to 6
- weight: bfloat16 [256, 256], replicated, may hold values from -0.375 to 0.375
- cotangent: bfloat16 [32768, 256], P(('row', 'col')), may hold values from -6 to 6
- tile_row: int32 [16, 16, 192], P('row', 'col'), may hold values from 0 to 15
- tile_col: int32 [16, 16, 192], P('row', 'col'), may hold values from 0 to 15
- tile_vals: bfloat16 [16, 16, 192, 128, 128], P('row', 'col'), may hold values from -0.0625 to 0.0625
- tile_count: int32 [16, 16], P('row', 'col'), may hold values from 1 to 192, as said below
Outputs:
- output: bfloat16 [32768, 256], P(('row', 'col'))
- weight_grad: float32 [256, 256], replicated
- feature_grad: bfloat16 [32768, 256], P(('col', 'row'))
Inputs may be any that keep to these rules, and one draw needn't show every extreme that they name: Only the first tile_count[p, q] slots of block (p, q) hold tiles; the other slots are ignored. Some block has all 192 slots live.
All inputs are finite; a program needn't handle non-finite values.
Results may differ from a plain program's by a relative error of at most 0.03.
Values may be sent and summed in bfloat16 or wider, within the bound.
A program may use at most 128 MiB of HBM per device.

v0:
```python
import jax
import jax.numpy as jnp
from jax import lax
from jax.sharding import PartitionSpec as P


def gelu_parts(pre_act):
    factor = 0.7978845608028654
    inner_arg = factor * (pre_act + 0.044715 * pre_act * pre_act * pre_act)
    tangent_h = jnp.tanh(inner_arg)
    activation = 0.5 * pre_act * (1.0 + tangent_h)
    gradient_slope = 0.5 * (1.0 + tangent_h) + 0.5 * pre_act * (
        1.0 - tangent_h * tangent_h
    ) * factor * (1.0 + 0.134145 * pre_act * pre_act)
    return (activation, gradient_slope)


def tile_product(tile_block, slot, source, source_at, backward):
    tile_size = tile_block.shape[-1]
    piece = lax.dynamic_slice_in_dim(source, source_at, tile_size, 0)
    if backward:
        return lax.dot_general(
            tile_block[slot], piece, (((0,), (0,)), ((), ())), preferred_element_type=jnp.float32
        )
    return jnp.dot(tile_block[slot], piece, preferred_element_type=jnp.float32)


def live_tiles(tile_block, row_ids, col_ids, live_count, source, out_rows, backward):
    tile_size = tile_block.shape[-1]
    feat_width = source.shape[1]
    source_ids = row_ids if backward else col_ids
    target_ids = col_ids if backward else row_ids

    def tile_step(slot, running):
        product = tile_product(tile_block, slot, source, source_ids[slot] * tile_size, backward)
        target = target_ids[slot] * tile_size
        current = lax.dynamic_slice_in_dim(running, target, tile_size, 0)
        return lax.dynamic_update_slice_in_dim(running, current + product, target, 0)

    start = jnp.zeros((out_rows, feat_width), jnp.float32)
    return lax.fori_loop(0, live_count, tile_step, start)


def tile_products(tile_block, row_ids, col_ids, live_count, source, out_rows, backward):
    return live_tiles(tile_block, row_ids, col_ids, live_count, source, out_rows, backward)


def body(features, weight, cotangent, tile_row, tile_col, tile_vals, tile_count):
    n_rows = lax.axis_size("row")
    n_cols = lax.axis_size("col")
    local_nodes = features.shape[0]
    row_block = local_nodes * n_cols
    col_block = local_nodes * n_rows
    node_total = local_nodes * n_rows * n_cols
    tile_block = tile_vals[0, 0]
    row_ids = tile_row[0, 0]
    col_ids = tile_col[0, 0]
    live_count = tile_count[0, 0]
    column_feats = lax.all_gather(features, "row", axis=0, tiled=True)
    partial_rows = tile_products(
        tile_block, row_ids, col_ids, live_count, column_feats, row_block, False
    )
    aggregated = lax.psum_scatter(
        partial_rows.astype(jnp.bfloat16), "col", scatter_dimension=0, tiled=True
    )
    pre_act = jnp.dot(aggregated, weight, preferred_element_type=jnp.float32)
    activation, gradient_slope = gelu_parts(pre_act)
    output = activation.astype(jnp.bfloat16)
    grad_pre = (cotangent.astype(jnp.float32) * gradient_slope).astype(jnp.bfloat16)
    weight_terms = lax.dot_general(
        aggregated, grad_pre, (((0,), (0,)), ((), ())), preferred_element_type=jnp.float32
    )
    weight_grad = lax.psum(weight_terms, ("row", "col")) * node_total ** (-0.5)
    grad_agg = lax.dot_general(
        grad_pre, weight, (((1,), (1,)), ((), ())), preferred_element_type=jnp.float32
    ).astype(jnp.bfloat16)
    row_agg = lax.all_gather(grad_agg, "col", axis=0, tiled=True)
    partial_cols = tile_products(tile_block, row_ids, col_ids, live_count, row_agg, col_block, True)
    feature_grad = lax.psum_scatter(
        partial_cols.astype(jnp.bfloat16), "row", scatter_dimension=0, tiled=True
    )
    return (output, weight_grad, feature_grad)


def solution(mesh):
    in_specs = (
        P(("col", "row"), None),
        P(),
        P(("row", "col"), None),
        P("row", "col", None),
        P("row", "col", None),
        P("row", "col", None, None, None),
        P("row", "col"),
    )
    out_specs = (P(("row", "col"), None), P(), P(("col", "row"), None))
    return jax.shard_map(body, mesh=mesh, in_specs=in_specs, out_specs=out_specs, check_vma=False)
```

profile of v0, /device:TPU:1, one launch (start us, length us, event | category | flops | bytes accessed | tf_op | source)
XLA Modules:
  0.0 1923.3 jit_solution(15070279507063547622)
XLA Ops:
  8.0 62.8 %all-gather.3.cloned.1.call-done = bf16[2048,256]{1,0:T(8,128)(2,1)} async-done(((bf16[128,256]{1,0:T(8,128)(2,1)}), bf16[2048,256]{1,0:T(8,128)(2,1)}) %all-gather.3.cloned.1.call-update) | async-done | bytes 1048592 | tf_op jit(solution)/shard_map/all_gather | solution.py:59
  70.9 213.7 %while.20 = (s32[]{:T(128)}, f32[2048,256]{1,0:T(8,128)S(1)}, s32[]{:T(128)}, s32[192]{0:T(256)S(1)}, bf16[192,128,128]{2,1,0:T(8,128)(2,1)}, /*index=5*/s32[192...) while((s32[]{:T(128)}, f32[2048,256]{1,0:T(8,128)S(1)}, ...), condition=%wide.region_1.0_spmd, body=%wide.region_0.0_spmd.sunk | while | flops 8421389 | bytes 360735 | solution.py:41
  284.6 1.1 convert_element_type.18
  285.7 656.0 %reduce-scatter.3.cloned.1.call-done = bf16[128,256]{1,0:T(8,128)(2,1)} async-done(((bf16[2048,256]{1,0:T(8,128)(2,1)}), bf16[128,256]{1,0:T(8,128)(2,1)}) %reduce-scatter.3.cloned.1.call-update) | async-done | bytes 65552 | tf_op jit(solution)/shard_map/reduce_scatter | solution.py:63
  941.7 1.7 fusion.16
  944.4 1.8 fusion.17
  946.2 76.7 %all-gather.5.cloned.1.call-done = bf16[2048,256]{1,0:T(8,128)(2,1)} async-done(((bf16[128,256]{1,0:T(8,128)(2,1)}), bf16[2048,256]{1,0:T(8,128)(2,1)}) %all-gather.5.cloned.1.call-update) | async-done | bytes 1048592 | tf_op jit(solution)/shard_map/all_gather | solution.py:77
  1023.0 216.2 %while.21 = (s32[]{:T(128)}, f32[2048,256]{1,0:T(8,128)S(1)}, s32[]{:T(128)}, s32[192]{0:T(256)S(1)}, bf16[192,128,128]{2,1,0:T(8,128)(2,1)}, /*index=5*/s32[192...) while((s32[]{:T(128)}, f32[2048,256]{1,0:T(8,128)S(1)}, ...), condition=%wide.region_5.0_spmd, body=%wide.region_4.0_spmd.sunk | while | flops 8421389 | bytes 360735 | solution.py:41
  1060.0 1.1 fusion.35
  1064.2 1.1 fusion.35
  1068.4 1.1 fusion.35
  1072.7 1.1 fusion.35
  1076.9 1.1 fusion.35
  1081.1 1.1 fusion.35
  1085.4 1.1 fusion.35
  1089.6 1.1 fusion.35
  1093.8 1.1 fusion.35
  1110.7 1.1 fusion.35
  1114.9 1.1 fusion.35
  1119.2 1.1 fusion.35
  1123.4 1.1 fusion.35
  1127.6 1.1 fusion.35
  1153.0 1.1 fusion.35
  1161.4 1.1 fusion.35
  1178.4 1.1 fusion.35
  1195.3 1.1 fusion.35
  1212.2 1.1 fusion.35
  1216.4 1.1 fusion.35
  1239.3 1.1 convert_element_type.23
  1240.4 47.4 %all-reduce.2.cloned.1.call-done = f32[256,256]{1,0:T(8,128)} async-done(((f32[256,256]{1,0:T(8,128)}), f32[256,256]{1,0:T(8,128)}) %all-reduce.2.cloned.1.call-update) | async-done | bytes 262160 | tf_op jit(solution)/shard_map/psum | solution.py:73
  1287.8 1.7 broadcast_multiply_fusion
  1289.4 627.4 %reduce-scatter.5.cloned.1.call-done = bf16[128,256]{1,0:T(8,128)(2,1)} async-done(((bf16[2048,256]{1,0:T(8,128)(2,1)}), bf16[128,256]{1,0:T(8,128)(2,1)}) %reduce-scatter.5.cloned.1.call-update) | async-done | bytes 65552 | tf_op jit(solution)/shard_map/reduce_scatter | solution.py:79
  (307 shorter events, 206.7 us)
Async XLA Ops:
  7.2 934.6 %copy-start = (bf16[256,256]{1,0:T(8,128)(2,1)S(1)}, bf16[256,256]{1,0:T(8,128)(2,1)}, u32[]{:S(2)}) copy-start(bf16[256,256]{1,0:T(8,128)(2,1)} %param.12) | copy-start | bytes 393220
  7.2 63.7 %copy-start.3 = (s32[1,1,192]{2,1,0:T(1,128)S(1)}, s32[1,1,192]{2,1,0:T(1,128)}, u32[]{:S(2)}) copy-start(s32[1,1,192]{2,1,0:T(1,128)} %param.15) | copy-start | bytes 2308
  7.2 63.7 %copy-start.2 = (s32[1,1,192]{2,1,0:T(1,128)S(1)}, s32[1,1,192]{2,1,0:T(1,128)}, u32[]{:S(2)}) copy-start(s32[1,1,192]{2,1,0:T(1,128)} %param.14) | copy-start | bytes 2308
  7.2 63.5 %all-gather.3.cloned.1.call-start = ((), (), s32[]{:S(2)}) async-start(), calls=%async_computation.2 | async-start | bytes 1114112 | tf_op jit(solution)/shard_map/all_gather | solution.py:59
  7.9 933.8 %reduce-scatter.3.cloned.1.call-start = ((), (), s32[]{:S(2)}) async-start(), calls=%async_computation.3 | async-start | bytes 1114112 | tf_op jit(solution)/shard_map/reduce_scatter | solution.py:63
  284.6 657.2 %copy-start.1 = (bf16[128,256]{1,0:T(8,128)(2,1)S(1)}, bf16[128,256]{1,0:T(8,128)(2,1)}, u32[]{:S(2)}) copy-start(bf16[128,256]{1,0:T(8,128)(2,1)} %param.13) | copy-start | bytes 196612
  285.7 737.2 %all-gather.5.cloned.1.call-start = ((), (), s32[]{:S(2)}) async-start(), calls=%async_computation.5 | async-start | bytes 1114112 | tf_op jit(solution)/shard_map/all_gather | solution.py:77
  944.3 343.4 %all-reduce.2.cloned.1.call-start = ((), (), s32[]{:S(2)}) async-start(), calls=%async_computation.4 | async-start | bytes 524288 | tf_op jit(solution)/shard_map/psum | solution.py:73
  946.1 970.7 %reduce-scatter.5.cloned.1.call-start = ((), (), s32[]{:S(2)}) async-start(), calls=%async_computation.6 | async-start | bytes 1114112 | tf_op jit(solution)/shard_map/reduce_scatter | solution.py:79
Sparse Core Ops, SparseCore 0:
  10.8 59.9 all-gather.2
  285.8 655.8 reduce-scatter.2
  944.4 78.4 all-gather.4
  1029.7 258.0 all-reduce.1
  1292.9 623.9 reduce-scatter.4
where the time goes:
time: 1950 us; the launch traced here: 1920 us
  waiting for transfers between devices  1470 us (75%)
  loops' own time  204 us (10%)
  local copies, waits for them, and re-layouts  120 us (6%)
  matrix products  110 us (6%)
    reduce_scatter x1, waiting for transfers between devices, body(): lax.psum_scatter(partial_rows.astype(jnp.bfloat16), 'col', scatter_dimens...  656 us
    reduce_scatter x1, waiting for transfers between devices, body(): lax.psum_scatter(partial_cols.astype(jnp.bfloat16), 'row', scatter_dimens...  627 us
    another operation x2, loops' own time, live_tiles(): return lax.fori_loop(0, live_count, tile_step, start)  204 us
    all_gather x1, waiting for transfers between devices, body(): row_agg = lax.all_gather(grad_agg, 'col', axis=0, tiled=True)  76.7 us
    all_gather x1, waiting for transfers between devices, body(): column_feats = lax.all_gather(features, 'row', axis=0, tiled=True)  62.8 us
    dynamic_slice x102, local copies, waits for them, and re-layouts, tile_step(): source_ids[slot] * tile_size  60.1 us
    dynamic_slice x102, local copies, waits for them, and re-layouts, tile_step(): target = target_ids[slot] * tile_size  59.9 us
    dot_general x51, matrix products, tile_product(): lax.dot_general(tile_block[slot], piece, (((0,), (0,)), ((), ())), prefer...  54.3 us
  transfers between devices with their start and end apart: 5, of which 5 were waited for; matrix products, arithmetic and copies ran while one was open for 6% of the time, Pallas kernels for 0%

commit v1 on v0

v1 whole, which is shorter than its diff:
```python
import functools

import jax
import jax.numpy as jnp
from jax import lax
from jax.experimental import pallas as pl
from jax.experimental.pallas import tpu as pltpu
from jax.sharding import PartitionSpec as P

MESH = pl.DeviceIdType.MESH
F32 = jnp.float32
BF16 = jnp.bfloat16
N_Y, N_X, N_ZL = 4, 4, 4
TILE, FEAT, SLOTS = 128, 256, 192
BLOCKS = 16


def gelu_parts(pre_act):
    factor = 0.7978845608028654
    square = pre_act * pre_act
    tangent_h = jnp.tanh(factor * (pre_act + 0.044715 * pre_act * square))
    half = 0.5 * (1.0 + tangent_h)
    activation = pre_act * half
    slope = half + 0.5 * pre_act * (1.0 - tangent_h * tangent_h) * factor * (1.0 + 0.134145 * square)
    return activation, slope


def copies():
    names = {}

    def number(*name):
        return names.setdefault(name, len(names))

    return number


N_COPIES = 96


def kernel(
    feat_ref, weight_ref, cot_ref, row_ref, col_ref, vals_ref, count_ref,
    out_ref, wgrad_ref, fgrad_ref,
    tiles, dense_sum, adj, adj_t, keys, index_v, prev_s, last_s,
    feats, part, recv_x, send_z, recv_z, row_agg,
    part_b, recv_c, send_y, recv_y, send_h, recv_h,
    wg, wg_recv_c, wg_v, wg_recv_y, wg_u, wg_recv_x, wg_t, wg_t2, wg_u2, wg_v2,
    load_sem, index_sem, send_sem, recv_sem,
):
    r, q = lax.axis_index("row"), lax.axis_index("col")
    c, y, zh = r % 2, (r // 2) % N_Y, r // (2 * N_Y)
    x, zl = q % N_X, q // N_X

    def at(y=y, c=c, zh=zh, x=x, zl=zl):
        return (zh * (2 * N_Y) + y * 2 + c, zl * N_X + x)

    def row_of(y=y, c=c, zh=zh):
        return at(y, c, zh)[0]

    def col_of(x=x, zl=zl):
        return at(x=x, zl=zl)[1]

    def plus(v, k):
        return (v + k) % 4

    core_peer, high_peer = at(c=1 - c), at(zh=1 - zh)
    y_peer = {k: at(y=plus(y, k)) for k in (1, 2, 3)}
    x_peer = {k: at(x=plus(x, k)) for k in (1, 2, 3)}
    z_peer = {k: at(zl=plus(zl, k)) for k in (1, 2, 3)}

    number = copies()

    def send(name, src, dst, peer):
        i = number(*name)
        pltpu.make_async_remote_copy(
            src_ref=src, dst_ref=dst, send_sem=send_sem.at[i], recv_sem=recv_sem.at[i],
            device_id=peer, device_id_type=MESH,
        ).start()
        pending.append((i, src, peer))

    def arrived(name, dst):
        i = number(*name)
        pltpu.make_async_remote_copy(
            src_ref=dst, dst_ref=dst, send_sem=send_sem.at[i], recv_sem=recv_sem.at[i],
            device_id=core_peer, device_id_type=MESH,
        ).wait_recv()

    pending = []

    load = pltpu.make_async_copy(vals_ref, tiles, load_sem.at[0])
    load.start()

    barrier = pltpu.get_barrier_semaphore()
    peers = [core_peer, high_peer] + [p[k] for p in (y_peer, x_peer, z_peer) for k in (1, 2, 3)]
    for peer in peers:
        pl.semaphore_signal(barrier, inc=1, device_id=peer, device_id_type=MESH)
    pl.semaphore_wait(barrier, len(peers))

    own = feats.at[r]
    send(("f_h",), feat_ref, own, high_peer)
    for k in (2, 1, 3):
        send(("f_y", k), feat_ref, own, y_peer[k])
    send(("f_c", 0, 0), feat_ref, own, core_peer)
    feats[r] = feat_ref[...]

    keys[...] = jnp.full(keys.shape, -1, jnp.int32)
    keys[0:1, 0:SLOTS] = row_ref[...] * BLOCKS + col_ref[...]
    key_row = jnp.broadcast_to(keys[0:1, :], (256, 256))
    key_col = key_row.T
    at_t = lax.broadcasted_iota(jnp.int32, (256, 256), 0)
    at_s = lax.broadcasted_iota(jnp.int32, (256, 256), 1)
    before = jnp.max(jnp.where((key_col == key_row) & (at_t < at_s), at_t, -1), axis=0, keepdims=True)
    newest = jnp.max(jnp.where((key_col == at_s) & (at_t < count_ref[0, 0]), at_t, -1), axis=0, keepdims=True)
    index_v[0] = jnp.where(before < 0, SLOTS, before)
    index_v[1] = jnp.where(newest < 0, SLOTS, newest)
    first = pltpu.make_async_copy(index_v.at[0], prev_s, index_sem.at[0])
    second = pltpu.make_async_copy(index_v.at[1], last_s, index_sem.at[1])
    first.start()
    second.start()
    first.wait()
    second.wait()
    load.wait()

    other = row_of(zh=1 - zh)
    arrived(("f_h",), feats.at[other])
    for k in (2, 1, 3):
        send(("f_hy", k), feats.at[other], feats.at[other], y_peer[k])
    send(("f_c", 1, 0), feats.at[other], feats.at[other], core_peer)

    dense_sum[SLOTS] = jnp.zeros((TILE, TILE), F32)

    def add_slot(s, carry):
        dense_sum[s] = dense_sum[jnp.clip(prev_s[0, s], 0, SLOTS)] + tiles[s].astype(F32)
        return carry

    lax.fori_loop(0, SLOTS, add_slot, 0)

    for k in (1, 3, 2):
        near = row_of(y=plus(y, -k))
        arrived(("f_y", k), feats.at[near])
        send(("f_c", 0, k), feats.at[near], feats.at[near], core_peer)

    def fill_row(i, carry):
        for j in range(BLOCKS):
            adj[i, :, j * TILE:(j + 1) * TILE] = dense_sum[jnp.clip(last_s[0, i * BLOCKS + j], 0, SLOTS)].astype(BF16)
        return carry

    lax.fori_loop(0, BLOCKS, fill_row, 0)

    for k in (1, 3, 2):
        far = row_of(y=plus(y, -k), zh=1 - zh)
        arrived(("f_hy", k), feats.at[far])
        send(("f_c", 1, k), feats.at[far], feats.at[far], core_peer)
    for h in (0, 1):
        for k in (0, 1, 3, 2):
            src = row_of(y=plus(y, -k), c=1 - c, zh=zh if h == 0 else 1 - zh)
            arrived(("f_c", h, k), feats.at[src])

    source = feats[...].reshape(BLOCKS * TILE, FEAT)
    for kz in (2, 1, 3, 0):
        to = plus(zl, kz)
        rows = adj[pl.ds(to * N_X, N_X)].reshape(N_X * TILE, BLOCKS * TILE)
        part[to] = jnp.dot(rows, source, preferred_element_type=F32).astype(BF16).reshape(N_X, TILE, FEAT)
        for kx in (2, 1, 3):
            send(("p_x", kx, kz), part.at[to, plus(x, kx)], recv_x.at[kx - 1, to], x_peer[kx])

    def turn_row(i, carry):
        for j in range(BLOCKS):
            adj_t[i, :, j * TILE:(j + 1) * TILE] = adj[j, :, pl.ds(pl.multiple_of(i * TILE, TILE), TILE)].T
        return carry

    lax.fori_loop(0, BLOCKS // 2, turn_row, 0)

    for kz in (2, 1, 3, 0):
        to = plus(zl, kz)
        for kx in (1, 3, 2):
            arrived(("p_x", kx, kz), recv_x.at[kx - 1, to])
        total = part[to, x].astype(F32) + recv_x[0, to].astype(F32) + recv_x[1, to].astype(F32) + recv_x[2, to].astype(F32)
        if kz:
            send_z[kz - 1] = total.astype(BF16)
            send(("p_z", kz), send_z.at[kz - 1], recv_z.at[kz - 1], z_peer[kz])

    lax.fori_loop(BLOCKS // 2, BLOCKS, turn_row, 0)

    for kz in (1, 3, 2):
        arrived(("p_z", kz), recv_z.at[kz - 1])
        total = total + recv_z[kz - 1].astype(F32)
    aggregated = total.astype(BF16)

    weight = weight_ref[...]
    pre_act = jnp.dot(aggregated, weight, preferred_element_type=F32)
    activation, slope = gelu_parts(pre_act)
    grad_pre = (cot_ref[...].astype(F32) * slope).astype(BF16)
    grad_agg = lax.dot_general(grad_pre, weight, (((1,), (1,)), ((), ())), preferred_element_type=F32)
    row_agg[q] = grad_agg.astype(BF16)

    own = row_agg.at[q]
    for kz in (2, 1, 3):
        send(("g_z", kz), own, own, z_peer[kz])
    for kx in (2, 1, 3):
        send(("g_x", 0, kx), own, own, x_peer[kx])
    out_ref[...] = activation.astype(BF16)
    wg[...] = lax.dot_general(
        aggregated, grad_pre, (((0,), (0,)), ((), ())), preferred_element_type=F32
    ).reshape(2, TILE, FEAT)
    send(("w_c",), wg.at[1 - c], wg_recv_c, core_peer)

    for kz in (1, 3, 2):
        near = col_of(zl=plus(zl, -kz))
        arrived(("g_z", kz), row_agg.at[near])
        for kx in (2, 1, 3):
            send(("g_x", kz, kx), row_agg.at[near], row_agg.at[near], x_peer[kx])

    arrived(("w_c",), wg_recv_c)
    wg_v[...] = (wg[c] + wg_recv_c[...]).reshape(N_Y, TILE // N_Y, FEAT)
    for k in (2, 1, 3):
        send(("w_y", k), wg_v.at[plus(y, k)], wg_recv_y.at[k - 1], y_peer[k])
    for kx in (1, 3, 2):
        arrived(("g_x", 0, kx), row_agg.at[col_of(x=plus(x, -kx))])
    for k in (1, 3, 2):
        arrived(("w_y", k), wg_recv_y.at[k - 1])
    wg_u[...] = (wg_v[y] + wg_recv_y[0] + wg_recv_y[1] + wg_recv_y[2]).reshape(N_X, 8, FEAT)
    for k in (2, 1, 3):
        send(("w_x", k), wg_u.at[plus(x, k)], wg_recv_x.at[k - 1], x_peer[k])

    for kz in (1, 3, 2):
        for kx in (1, 3, 2):
            arrived(("g_x", kz, kx), row_agg.at[col_of(x=plus(x, -kx), zl=plus(zl, -kz))])

    source_b = row_agg[...].reshape(BLOCKS * TILE, FEAT)

    def backward(to_c, to_h, dst):
        for j in range(N_Y):
            rows = adj_t[to_h * (2 * N_Y) + j * 2 + to_c]
            dst[j] = jnp.dot(rows, source_b, preferred_element_type=F32).astype(BF16)

    for i, (to_c, to_h) in enumerate(((1 - c, 1 - zh), (1 - c, zh), (c, 1 - zh), (c, zh))):
        backward(to_c, to_h, part_b.at[i])
        if i < 2:
            send(("b_c", i), part_b.at[i], recv_c.at[i], core_peer)
        if i == 1:
            for k in (1, 3, 2):
                arrived(("w_x", k), wg_recv_x.at[k - 1])
            wg_t[zl] = wg_u[x] + wg_recv_x[0] + wg_recv_x[1] + wg_recv_x[2]
            for k in (2, 1, 3):
                send(("w_z", k), wg_t.at[zl], wg_t.at[zl], z_peer[k])
        if i >= 2:
            h = i - 2
            arrived(("b_c", h), recv_c.at[h])
            send_y[h] = (part_b[i].astype(F32) + recv_c[h].astype(F32)).astype(BF16)
            for k in (2, 1, 3):
                send(("b_y", h, k), send_y.at[h, plus(y, k)], recv_y.at[h, k - 1], y_peer[k])

    for k in (1, 3, 2):
        arrived(("w_z", k), wg_t.at[plus(zl, -k)])
    wg_t2[zh] = (wg_t[0] + wg_t[1]) + (wg_t[2] + wg_t[3])
    send(("w_h",), wg_t2.at[zh], wg_t2.at[zh], high_peer)

    for h in (0, 1):
        for k in (1, 3, 2):
            arrived(("b_y", h, k), recv_y.at[h, k - 1])
        total = send_y[h, y].astype(F32) + recv_y[h, 0].astype(F32) + recv_y[h, 1].astype(F32) + recv_y[h, 2].astype(F32)
        if h == 0:
            send_h[...] = total.astype(BF16)
            send(("b_h",), send_h, recv_h, high_peer)

    arrived(("w_h",), wg_t2.at[1 - zh])
    wg_u2[x] = wg_t2[0] + wg_t2[1]
    for k in (2, 1, 3):
        send(("w_xb", k), wg_u2.at[x], wg_u2.at[x], x_peer[k])
    for k in (1, 3, 2):
        arrived(("w_xb", k), wg_u2.at[plus(x, -k)])
    wg_v2[y] = wg_u2[...].reshape(TILE // N_Y, FEAT)
    for k in (2, 1, 3):
        send(("w_yb", k), wg_v2.at[y], wg_v2.at[y], y_peer[k])

    arrived(("b_h",), recv_h)
    fgrad_ref[...] = (total + recv_h[...].astype(F32)).astype(BF16)

    for k in (1, 3, 2):
        arrived(("w_yb", k), wg_v2.at[plus(y, -k)])
    wgrad_ref[c] = wg_v2[...].reshape(TILE, FEAT)
    send(("w_cb",), wgrad_ref.at[c], wgrad_ref.at[c], core_peer)
    arrived(("w_cb",), wgrad_ref.at[1 - c])

    for i, src, peer in pending:
        pltpu.make_async_remote_copy(
            src_ref=src, dst_ref=src, send_sem=send_sem.at[i], recv_sem=recv_sem.at[i],
            device_id=peer, device_id_type=MESH,
        ).wait_send()


def body(features, weight, cotangent, tile_row, tile_col, tile_vals, tile_count):
    node_total = 32768
    vmem, smem = pl.BlockSpec(memory_space=pltpu.VMEM), pl.BlockSpec(memory_space=pltpu.SMEM)
    output, weight_sum, feature_grad = pl.pallas_call(
        kernel,
        out_shape=(
            jax.ShapeDtypeStruct((TILE, FEAT), BF16),
            jax.ShapeDtypeStruct((2, TILE, FEAT), F32),
            jax.ShapeDtypeStruct((TILE, FEAT), BF16),
        ),
        in_specs=[vmem, vmem, vmem, vmem, vmem, pl.BlockSpec(memory_space=pl.ANY), smem],
        out_specs=(vmem, vmem, vmem),
        scratch_shapes=[
            pltpu.VMEM((SLOTS, TILE, TILE), BF16),
            pltpu.VMEM((SLOTS + 1, TILE, TILE), F32),
            pltpu.VMEM((BLOCKS, TILE, BLOCKS * TILE), BF16),
            pltpu.VMEM((BLOCKS, TILE, BLOCKS * TILE), BF16),
            pltpu.VMEM((8, 256), jnp.int32),
            pltpu.VMEM((2, 1, 256), jnp.int32),
            pltpu.SMEM((1, 256), jnp.int32),
            pltpu.SMEM((1, 256), jnp.int32),
            pltpu.VMEM((BLOCKS, TILE, FEAT), BF16),
            pltpu.VMEM((N_ZL, N_X, TILE, FEAT), BF16),
            pltpu.VMEM((3, N_ZL, TILE, FEAT), BF16),
            pltpu.VMEM((3, TILE, FEAT), BF16),
            pltpu.VMEM((3, TILE, FEAT), BF16),
            pltpu.VMEM((BLOCKS, TILE, FEAT), BF16),
            pltpu.VMEM((4, N_Y, TILE, FEAT), BF16),
            pltpu.VMEM((2, N_Y, TILE, FEAT), BF16),
            pltpu.VMEM((2, N_Y, TILE, FEAT), BF16),
            pltpu.VMEM((2, 3, TILE, FEAT), BF16),
            pltpu.VMEM((TILE, FEAT), BF16),
            pltpu.VMEM((TILE, FEAT), BF16),
            pltpu.VMEM((2, TILE, FEAT), F32),
            pltpu.VMEM((TILE, FEAT), F32),
            pltpu.VMEM((N_Y, TILE // N_Y, FEAT), F32),
            pltpu.VMEM((3, TILE // N_Y, FEAT), F32),
            pltpu.VMEM((N_X, 8, FEAT), F32),
            pltpu.VMEM((3, 8, FEAT), F32),
            pltpu.VMEM((N_ZL, 8, FEAT), F32),
            pltpu.VMEM((2, 8, FEAT), F32),
            pltpu.VMEM((N_X, 8, FEAT), F32),
            pltpu.VMEM((N_Y, TILE // N_Y, FEAT), F32),
            pltpu.SemaphoreType.DMA((1,)),
            pltpu.SemaphoreType.DMA((2,)),
            pltpu.SemaphoreType.DMA((N_COPIES,)),
            pltpu.SemaphoreType.DMA((N_COPIES,)),
        ],
        compiler_params=pltpu.CompilerParams(
            collective_id=0, has_side_effects=True, vmem_limit_bytes=60 * 1024 * 1024
        ),
        name="layer",
    )(features, weight, cotangent, tile_row[0], tile_col[0], tile_vals[0, 0], tile_count)
    weight_grad = weight_sum.reshape(FEAT, FEAT) * node_total ** (-0.5)
    return output, weight_grad, feature_grad


def solution(mesh):
    in_specs = (
        P(("col", "row"), None),
        P(),
        P(("row", "col"), None),
        P("row", "col", None),
        P("row", "col", None),
        P("row", "col", None, None, None),
        P("row", "col"),
    )
    out_specs = (P(("row", "col"), None), P(), P(("col", "row"), None))
    return jax.shard_map(body, mesh=mesh, in_specs=in_specs, out_specs=out_specs, check_vma=False)
```

time: 1950 us -> 83.8 us (0.04); the launches traced: 1920 us -> 83.5 us
  waiting for transfers between devices: 1470 us -> 0 us
  loops' own time: 204 us -> 0 us
  local copies, waits for them, and re-layouts: 120 us -> 2.94 us
  matrix products: 110 us -> 0 us
  Pallas kernels: 0 us -> 77.6 us
    reduce_scatter x2 -> x0, waiting for transfers between devices: 1280 us -> none  [the longest x1 656 us: body(): lax.psum_scatter(partial_rows.astype(jnp.bfloat16), 'col', scatter_dimens...]
    another operation x2 -> x0, loops' own time: 204 us -> none  [live_tiles(): return lax.fori_loop(0, live_count, tile_step, start)]
    all_gather x2 -> x0, waiting for transfers between devices: 139 us -> none  [the longest x1 76.7 us: body(): row_agg = lax.all_gather(grad_agg, 'col', axis=0, tiled=True)]
    dynamic_slice x204 -> x0, local copies, waits for them, and re-layouts: 120 us -> none  [the longest x102 60.1 us: tile_step(): source_ids[slot] * tile_size]
    dot_general x105 -> x0, matrix products: 110 us -> none  [the longest x51 54.3 us: tile_product(): lax.dot_general(tile_block[slot], piece, (((0,), (0,)), ((), ())), prefer...]
    pallas_call x0 -> x1, Pallas kernels: none -> 77.6 us  [body(): pl.pallas_call(kernel, out_shape=(jax.ShapeDtypeStruct((TILE, FEAT), BF16...]
    psum x1 -> x0, waiting for transfers between devices: 47.4 us -> none  [body(): weight_grad = lax.psum(weight_terms, ('row', 'col')) * node_total ** (-0.5)]
  transfers between devices with their start and end apart: 5 -> 0, of which waited for: 5 -> 0; matrix products, arithmetic and copies ran while one was open for 6% -> 0% of each run, Pallas kernels for 0% -> 0%
where the time goes in v1:
time: 83.8 us; the launch traced here: 83.5 us
  Pallas kernels  77.6 us (93%)
  local copies, waits for them, and re-layouts  2.94 us (4%)
  other arithmetic  1.68 us (2%)
  between operations  1.29 us (2%)
    pallas_call x1, Pallas kernels, body(): pl.pallas_call(kernel, out_shape=(jax.ShapeDtypeStruct((TILE, FEAT), BF16...  77.6 us
    unnamed x2, local copies, waits for them, and re-layouts  2.94 us
    mul x1, other arithmetic, body(): weight_grad = weight_sum.reshape(FEAT, FEAT) * node_total ** (-0.5)  1.68 us

profile of v1, /device:TPU:1, one launch (start us, length us, event | category | flops | bytes accessed | tf_op | source)
XLA Modules:
  0.0 83.5 jit_solution(2093691214421988877)
XLA Ops:
  1.3 77.6 %layer.1 = (bf16[128,256]{1,0:T(8,128)(2,1)}, f32[2,128,256]{2,1,0:T(8,128)}, bf16[128,256]{1,0:T(8,128)(2,1)}) custom-call(bf16[128,256]{1,0:T(8,128)(2,1)} %feat_ref.1, bf16[256,256]{1,0:T(8,128)(2,1)} %weight_ref.1, bf16[128,256]{1,0:T(8,128)(2,1)} %cot_ref.1, s32[1,192]{1,0:T(1,128)} %bitcast.6, s32[1,192]{1,0:T(1,128)} %bitcast.7, ...), custom_call_target="tpu_custom_call" | custom-call | tf_op jit(solution)/shard_map/layer/pallas_call | solution.py:295
  78.9 1.7 %broadcast_multiply_fusion = f32[2,128,256]{2,1,0:T(8,128)} fusion(f32[2,128,256]{2,1,0:T(8,128)} %get-tuple-element.7), kind=kLoop, calls=%fused_computation | loop fusion | flops 65536 | bytes 524288 | tf_op jit(solution)/shard_map/mul | solution.py:345
  80.5 1.5 %copy.13 = bf16[128,256]{1,0:T(8,128)(2,1)} copy(bf16[128,256]{1,0:T(8,128)(2,1)} %get-tuple-element.12) | data formatting | bytes 131072
  82.0 1.5 %copy.14 = bf16[128,256]{1,0:T(8,128)(2,1)} copy(bf16[128,256]{1,0:T(8,128)(2,1)} %get-tuple-element.14) | data formatting | bytes 131072

commit v2 on v1

--- a/solution.py
+++ b/solution.py
@@ -38,12 +38,13 @@
 
 
 def kernel(
-    feat_ref, weight_ref, cot_ref, row_ref, col_ref, vals_ref, count_ref,
+    scale, feat_ref, weight_hbm, cot_hbm, row_hbm, col_hbm, vals_ref, count_hbm,
     out_ref, wgrad_ref, fgrad_ref,
+    weight_ref, cot_ref, row_ref, col_ref, count_ref,
     tiles, dense_sum, adj, adj_t, keys, index_v, prev_s, last_s,
     feats, part, recv_x, send_z, recv_z, row_agg,
     part_b, recv_c, send_y, recv_y, send_h, recv_h,
-    wg, wg_recv_c, wg_v, wg_recv_y, wg_u, wg_recv_x, wg_t, wg_t2, wg_u2, wg_v2,
+    wg, wg_recv_c, wg_v, wg_recv_y, wg_u, wg_recv_z, wg_t, wg_t2, wg_u2, wg_v2,
     load_sem, index_sem, send_sem, recv_sem,
 ):
     r, q = lax.axis_index("row"), lax.axis_index("col")
@@ -86,8 +87,14 @@
 
     pending = []
 
-    load = pltpu.make_async_copy(vals_ref, tiles, load_sem.at[0])
-    load.start()
+    own = feats.at[r]
+    loads = {}
+    for i, (src, dst) in enumerate((
+        (row_hbm, row_ref), (col_hbm, col_ref), (count_hbm, count_ref), (feat_ref, own),
+        (weight_hbm, weight_ref), (cot_hbm, cot_ref), (vals_ref, tiles),
+    )):
+        loads[i] = pltpu.make_async_copy(src, dst, load_sem.at[i])
+        loads[i].start()
 
     barrier = pltpu.get_barrier_semaphore()
     peers = [core_peer, high_peer] + [p[k] for p in (y_peer, x_peer, z_peer) for k in (1, 2, 3)]
@@ -95,13 +102,13 @@
         pl.semaphore_signal(barrier, inc=1, device_id=peer, device_id_type=MESH)
     pl.semaphore_wait(barrier, len(peers))
 
-    own = feats.at[r]
     send(("f_h",), feat_ref, own, high_peer)
     for k in (2, 1, 3):
         send(("f_y", k), feat_ref, own, y_peer[k])
     send(("f_c", 0, 0), feat_ref, own, core_peer)
-    feats[r] = feat_ref[...]
-
+
+    for i in range(3):
+        loads[i].wait()
     keys[...] = jnp.full(keys.shape, -1, jnp.int32)
     keys[0:1, 0:SLOTS] = row_ref[...] * BLOCKS + col_ref[...]
     key_row = jnp.broadcast_to(keys[0:1, :], (256, 256))
@@ -118,7 +125,8 @@
     second.start()
     first.wait()
     second.wait()
-    load.wait()
+    for i in range(3, 7):
+        loads[i].wait()
 
     other = row_of(zh=1 - zh)
     arrived(("f_h",), feats.at[other])
@@ -209,22 +217,26 @@
         arrived(("g_z", kz), row_agg.at[near])
         for kx in (2, 1, 3):
             send(("g_x", kz, kx), row_agg.at[near], row_agg.at[near], x_peer[kx])
-
-    arrived(("w_c",), wg_recv_c)
-    wg_v[...] = (wg[c] + wg_recv_c[...]).reshape(N_Y, TILE // N_Y, FEAT)
+        if kz == 1:
+            arrived(("w_c",), wg_recv_c)
+            wg_v[...] = (wg[c] + wg_recv_c[...]).reshape(N_Y, TILE // N_Y, FEAT)
+            for k in (2, 1, 3):
+                send(("w_y", k), wg_v.at[plus(y, k)], wg_recv_y.at[k - 1], y_peer[k])
+
+    for k in (1, 3, 2):
+        arrived(("w_y", k), wg_recv_y.at[k - 1])
+    wg_u[...] = (wg_v[y] + wg_recv_y[0] + wg_recv_y[1] + wg_recv_y[2]).reshape(N_ZL, 8, FEAT)
     for k in (2, 1, 3):
-        send(("w_y", k), wg_v.at[plus(y, k)], wg_recv_y.at[k - 1], y_peer[k])
-    for kx in (1, 3, 2):
-        arrived(("g_x", 0, kx), row_agg.at[col_of(x=plus(x, -kx))])
-    for k in (1, 3, 2):
-        arrived(("w_y", k), wg_recv_y.at[k - 1])
-    wg_u[...] = (wg_v[y] + wg_recv_y[0] + wg_recv_y[1] + wg_recv_y[2]).reshape(N_X, 8, FEAT)
-    for k in (2, 1, 3):
-        send(("w_x", k), wg_u.at[plus(x, k)], wg_recv_x.at[k - 1], x_peer[k])
-
-    for kz in (1, 3, 2):
+        send(("w_z", k), wg_u.at[plus(zl, k)], wg_recv_z.at[k - 1], z_peer[k])
+
+    for kz in (0, 1, 3, 2):
         for kx in (1, 3, 2):
             arrived(("g_x", kz, kx), row_agg.at[col_of(x=plus(x, -kx), zl=plus(zl, -kz))])
+        if kz == 1:
+            for k in (1, 3, 2):
+                arrived(("w_z", k), wg_recv_z.at[k - 1])
+            wg_t[zh] = wg_u[zl] + wg_recv_z[0] + wg_recv_z[1] + wg_recv_z[2]
+            send(("w_h",), wg_t.at[zh], wg_t.at[zh], high_peer)
 
     source_b = row_agg[...].reshape(BLOCKS * TILE, FEAT)
 
@@ -233,27 +245,27 @@
             rows = adj_t[to_h * (2 * N_Y) + j * 2 + to_c]
             dst[j] = jnp.dot(rows, source_b, preferred_element_type=F32).astype(BF16)
 
-    for i, (to_c, to_h) in enumerate(((1 - c, 1 - zh), (1 - c, zh), (c, 1 - zh), (c, zh))):
+    for i, (to_c, to_h) in enumerate(((1 - c, 1 - zh), (c, 1 - zh), (1 - c, zh), (c, zh))):
         backward(to_c, to_h, part_b.at[i])
-        if i < 2:
-            send(("b_c", i), part_b.at[i], recv_c.at[i], core_peer)
-        if i == 1:
-            for k in (1, 3, 2):
-                arrived(("w_x", k), wg_recv_x.at[k - 1])
-            wg_t[zl] = wg_u[x] + wg_recv_x[0] + wg_recv_x[1] + wg_recv_x[2]
-            for k in (2, 1, 3):
-                send(("w_z", k), wg_t.at[zl], wg_t.at[zl], z_peer[k])
-        if i >= 2:
-            h = i - 2
+        h = i // 2
+        if i in (0, 2):
+            send(("b_c", h), part_b.at[i], recv_c.at[h], core_peer)
+        else:
             arrived(("b_c", h), recv_c.at[h])
             send_y[h] = (part_b[i].astype(F32) + recv_c[h].astype(F32)).astype(BF16)
             for k in (2, 1, 3):
                 send(("b_y", h, k), send_y.at[h, plus(y, k)], recv_y.at[h, k - 1], y_peer[k])
-
-    for k in (1, 3, 2):
-        arrived(("w_z", k), wg_t.at[plus(zl, -k)])
-    wg_t2[zh] = (wg_t[0] + wg_t[1]) + (wg_t[2] + wg_t[3])
-    send(("w_h",), wg_t2.at[zh], wg_t2.at[zh], high_peer)
+        if i == 0:
+            arrived(("w_h",), wg_t.at[1 - zh])
+            wg_t2[x] = wg_t[0] + wg_t[1]
+            for k in (2, 1, 3):
+                send(("w_x", k), wg_t2.at[x], wg_t2.at[x], x_peer[k])
+
+    for k in (1, 3, 2):
+        arrived(("w_x", k), wg_t2.at[plus(x, -k)])
+    wg_u2[zl] = ((wg_t2[0] + wg_t2[1]) + (wg_t2[2] + wg_t2[3])) * scale
+    for k in (2, 1, 3):
+        send(("w_zb", k), wg_u2.at[zl], wg_u2.at[zl], z_peer[k])
 
     for h in (0, 1):
         for k in (1, 3, 2):
@@ -262,24 +274,19 @@
         if h == 0:
             send_h[...] = total.astype(BF16)
             send(("b_h",), send_h, recv_h, high_peer)
-
-    arrived(("w_h",), wg_t2.at[1 - zh])
-    wg_u2[x] = wg_t2[0] + wg_t2[1]
-    for k in (2, 1, 3):
-        send(("w_xb", k), wg_u2.at[x], wg_u2.at[x], x_peer[k])
-    for k in (1, 3, 2):
-        arrived(("w_xb", k), wg_u2.at[plus(x, -k)])
-    wg_v2[y] = wg_u2[...].reshape(TILE // N_Y, FEAT)
-    for k in (2, 1, 3):
-        send(("w_yb", k), wg_v2.at[y], wg_v2.at[y], y_peer[k])
-
-    arrived(("b_h",), recv_h)
-    fgrad_ref[...] = (total + recv_h[...].astype(F32)).astype(BF16)
+            for k in (1, 3, 2):
+                arrived(("w_zb", k), wg_u2.at[plus(zl, -k)])
+            wg_v2[y] = wg_u2[...].reshape(TILE // N_Y, FEAT)
+            for k in (2, 1, 3):
+                send(("w_yb", k), wg_v2.at[y], wg_v2.at[y], y_peer[k])
 
     for k in (1, 3, 2):
         arrived(("w_yb", k), wg_v2.at[plus(y, -k)])
     wgrad_ref[c] = wg_v2[...].reshape(TILE, FEAT)
     send(("w_cb",), wgrad_ref.at[c], wgrad_ref.at[c], core_peer)
+
+    arrived(("b_h",), recv_h)
+    fgrad_ref[...] = (total + recv_h[...].astype(F32)).astype(BF16)
     arrived(("w_cb",), wgrad_ref.at[1 - c])
 
     for i, src, peer in pending:
@@ -289,19 +296,34 @@
         ).wait_send()
 
 
+def hand_over(out_src, wgrad_src, fgrad_src, out_dst, wgrad_dst, fgrad_dst, sem):
+    pairs = ((out_src, out_dst), (wgrad_src, wgrad_dst), (fgrad_src, fgrad_dst))
+    moves = [pltpu.make_async_copy(src, dst, sem.at[i]) for i, (src, dst) in enumerate(pairs)]
+    for move in moves:
+        move.start()
+    for move in moves:
+        move.wait()
+
+
 def body(features, weight, cotangent, tile_row, tile_col, tile_vals, tile_count):
-    node_total = 32768
-    vmem, smem = pl.BlockSpec(memory_space=pltpu.VMEM), pl.BlockSpec(memory_space=pltpu.SMEM)
-    output, weight_sum, feature_grad = pl.pallas_call(
-        kernel,
-        out_shape=(
-            jax.ShapeDtypeStruct((TILE, FEAT), BF16),
-            jax.ShapeDtypeStruct((2, TILE, FEAT), F32),
-            jax.ShapeDtypeStruct((TILE, FEAT), BF16),
-        ),
-        in_specs=[vmem, vmem, vmem, vmem, vmem, pl.BlockSpec(memory_space=pl.ANY), smem],
-        out_specs=(vmem, vmem, vmem),
+    whole = pl.BlockSpec(memory_space=pl.ANY)
+    scale = (BLOCKS * BLOCKS * TILE) ** -0.5
+    out_shape = (
+        jax.ShapeDtypeStruct((TILE, FEAT), BF16),
+        jax.ShapeDtypeStruct((2, TILE, FEAT), F32),
+        jax.ShapeDtypeStruct((TILE, FEAT), BF16),
+    )
+    results = pl.pallas_call(
+        functools.partial(kernel, scale),
+        out_shape=out_shape,
+        in_specs=[whole] * 7,
+        out_specs=(pl.BlockSpec(memory_space=pltpu.VMEM),) * 3,
         scratch_shapes=[
+            pltpu.VMEM((FEAT, FEAT), BF16),
+            pltpu.VMEM((TILE, FEAT), BF16),
+            pltpu.VMEM((1, SLOTS), jnp.int32),
+            pltpu.VMEM((1, SLOTS), jnp.int32),
+            pltpu.SMEM((1, 1), jnp.int32),
             pltpu.VMEM((SLOTS, TILE, TILE), BF16),
             pltpu.VMEM((SLOTS + 1, TILE, TILE), F32),
             pltpu.VMEM((BLOCKS, TILE, BLOCKS * TILE), BF16),
@@ -326,24 +348,31 @@
             pltpu.VMEM((TILE, FEAT), F32),
             pltpu.VMEM((N_Y, TILE // N_Y, FEAT), F32),
             pltpu.VMEM((3, TILE // N_Y, FEAT), F32),
-            pltpu.VMEM((N_X, 8, FEAT), F32),
+            pltpu.VMEM((N_ZL, 8, FEAT), F32),
             pltpu.VMEM((3, 8, FEAT), F32),
-            pltpu.VMEM((N_ZL, 8, FEAT), F32),
             pltpu.VMEM((2, 8, FEAT), F32),
             pltpu.VMEM((N_X, 8, FEAT), F32),
+            pltpu.VMEM((N_ZL, 8, FEAT), F32),
             pltpu.VMEM((N_Y, TILE // N_Y, FEAT), F32),
-            pltpu.SemaphoreType.DMA((1,)),
+            pltpu.SemaphoreType.DMA((10,)),
             pltpu.SemaphoreType.DMA((2,)),
             pltpu.SemaphoreType.DMA((N_COPIES,)),
             pltpu.SemaphoreType.DMA((N_COPIES,)),
         ],
         compiler_params=pltpu.CompilerParams(
-            collective_id=0, has_side_effects=True, vmem_limit_bytes=60 * 1024 * 1024
+            collective_id=0, has_side_effects=True, vmem_limit_bytes=62 * 1024 * 1024
         ),
         name="layer",
     )(features, weight, cotangent, tile_row[0], tile_col[0], tile_vals[0, 0], tile_count)
-    weight_grad = weight_sum.reshape(FEAT, FEAT) * node_total ** (-0.5)
-    return output, weight_grad, feature_grad
+    output, weight_grad, feature_grad = pl.pallas_call(
+        hand_over,
+        out_shape=out_shape,
+        in_specs=[pl.BlockSpec(memory_space=pltpu.VMEM)] * 3,
+        out_specs=(whole,) * 3,
+        scratch_shapes=[pltpu.SemaphoreType.DMA((3,))],
+        name="hand_over",
+    )(*results)
+    return output, weight_grad.reshape(FEAT, FEAT), feature_grad
 
 
 def solution(mesh):

time: 83.8 us -> 75.5 us (0.901)
  Pallas kernels: 77.6 us -> 74.1 us
  local copies, waits for them, and re-layouts: 2.94 us -> 0 us
  other arithmetic: 1.68 us -> 0 us
    pallas_call x1 -> x2, Pallas kernels: 77.6 us -> 74.1 us  [the longest x1 72.4 us: body(): pl.pallas_call(functools.partial(kernel, scale), out_shape=out_shape, in_...]
    unnamed x2 -> x0, local copies, waits for them, and re-layouts: 2.94 us -> none
    mul x1 -> x0, other arithmetic: 1.68 us -> none  [body(): weight_grad = weight_sum.reshape(FEAT, FEAT) * node_total ** (-0.5)]
where the time goes in v2:
time: 75.5 us; the launch traced here: 75.4 us
  Pallas kernels  74.1 us (98%)
  between operations  1.29 us (2%)
    pallas_call x1, Pallas kernels, body(): pl.pallas_call(functools.partial(kernel, scale), out_shape=out_shape, in_...  72.4 us
    pallas_call x1, Pallas kernels, body(): pl.pallas_call(hand_over, out_shape=out_shape, in_specs=[pl.BlockSpec(mem...  1.71 us

profile of v2, /device:TPU:1, one launch (start us, length us, event | category | flops | bytes accessed | tf_op | source)
XLA Modules:
  0.0 75.4 jit_solution(3097050951781013740)
XLA Ops:
  1.3 72.4 %layer.1 = (bf16[128,256]{1,0:T(8,128)(2,1)}, f32[2,128,256]{2,1,0:T(8,128)}, bf16[128,256]{1,0:T(8,128)(2,1)}) custom-call(bf16[128,256]{1,0:T(8,128)(2,1)} %feat_ref.1, bf16[256,256]{1,0:T(8,128)(2,1)} %weight_hbm.1, bf16[128,256]{1,0:T(8,128)(2,1)} %cot_hbm.1, s32[1,192]{1,0:T(1,128)} %bitcast.5, s32[1,192]{1,0:T(1,128)} %bitcast.6, ...), custom_call_target="tpu_custom_call" | custom-call | tf_op jit(solution)/shard_map/layer/pallas_call | solution.py:316
  73.6 1.7 %hand_over.1 = (bf16[128,256]{1,0:T(8,128)(2,1)}, f32[2,128,256]{2,1,0:T(8,128)}, bf16[128,256]{1,0:T(8,128)(2,1)}) custom-call(bf16[128,256]{1,0:T(8,128)(2,1)} %get-tuple-element.9.out_src, f32[2,128,256]{2,1,0:T(8,128)} %get-tuple-element.10.wgrad_src, bf16[128,256]{1,0:T(8,128)(2,1)} %get-tuple-element.11.fgrad_src), custom_call_target="tpu_custom_call" | custom-call | tf_op jit(solution)/shard_map/hand_over/pallas_call | solution.py:367

commit v3 on v2

--- a/solution.py
+++ b/solution.py
@@ -13,6 +13,7 @@
 N_Y, N_X, N_ZL = 4, 4, 4
 TILE, FEAT, SLOTS = 128, 256, 192
 BLOCKS = 16
+SPLIT = 64
 
 
 def gelu_parts(pre_act):
@@ -34,7 +35,7 @@
     return number
 
 
-N_COPIES = 96
+N_COPIES = 104
 
 
 def kernel(
@@ -44,7 +45,7 @@
     tiles, dense_sum, adj, adj_t, keys, index_v, prev_s, last_s,
     feats, part, recv_x, send_z, recv_z, row_agg,
     part_b, recv_c, send_y, recv_y, send_h, recv_h,
-    wg, wg_recv_c, wg_v, wg_recv_y, wg_u, wg_recv_z, wg_t, wg_t2, wg_u2, wg_v2,
+    wg, wg_recv_c, wg_v, wg_recv_y, wg_u, wg_recv_z, wg_t, wg_t2, wg_u2, wg_v2, grown,
     load_sem, index_sem, send_sem, recv_sem,
 ):
     r, q = lax.axis_index("row"), lax.axis_index("col")
@@ -163,17 +164,16 @@
             src = row_of(y=plus(y, -k), c=1 - c, zh=zh if h == 0 else 1 - zh)
             arrived(("f_c", h, k), feats.at[src])
 
-    source = feats[...].reshape(BLOCKS * TILE, FEAT)
     for kz in (2, 1, 3, 0):
         to = plus(zl, kz)
         rows = adj[pl.ds(to * N_X, N_X)].reshape(N_X * TILE, BLOCKS * TILE)
-        part[to] = jnp.dot(rows, source, preferred_element_type=F32).astype(BF16).reshape(N_X, TILE, FEAT)
+        part[to] = jnp.dot(rows, feats[...].reshape(BLOCKS * TILE, FEAT), preferred_element_type=F32).astype(BF16).reshape(N_X, TILE, FEAT)
         for kx in (2, 1, 3):
             send(("p_x", kx, kz), part.at[to, plus(x, kx)], recv_x.at[kx - 1, to], x_peer[kx])
 
     def turn_row(i, carry):
         for j in range(BLOCKS):
-            adj_t[i, :, j * TILE:(j + 1) * TILE] = adj[j, :, pl.ds(pl.multiple_of(i * TILE, TILE), TILE)].T
+            adj_t[(i % 2) * (BLOCKS // 2) + i // 2, :, j * TILE:(j + 1) * TILE] = adj[j, :, pl.ds(pl.multiple_of(i * TILE, TILE), TILE)].T
         return carry
 
     lax.fori_loop(0, BLOCKS // 2, turn_row, 0)
@@ -212,16 +212,22 @@
     ).reshape(2, TILE, FEAT)
     send(("w_c",), wg.at[1 - c], wg_recv_c, core_peer)
 
+    arrived(("w_c",), wg_recv_c)
+    wg_v[...] = (wg[c] + wg_recv_c[...]).reshape(N_Y, TILE // N_Y, FEAT)
+    for k in (2, 1, 3):
+        send(("w_y", k), wg_v.at[plus(y, k)], wg_recv_y.at[k - 1], y_peer[k])
     for kz in (1, 3, 2):
         near = col_of(zl=plus(zl, -kz))
         arrived(("g_z", kz), row_agg.at[near])
-        for kx in (2, 1, 3):
+        for kx in (1, 3):
             send(("g_x", kz, kx), row_agg.at[near], row_agg.at[near], x_peer[kx])
+        piece = row_agg.at[near, pl.ds(0, SPLIT)]
+        send(("g_x", kz, 2), piece, piece, x_peer[2])
         if kz == 1:
-            arrived(("w_c",), wg_recv_c)
-            wg_v[...] = (wg[c] + wg_recv_c[...]).reshape(N_Y, TILE // N_Y, FEAT)
+            arrived(("g_x", 0, 2), row_agg.at[col_of(x=plus(x, 2))])
+            piece = row_agg.at[col_of(x=plus(x, 2)), pl.ds(SPLIT, TILE - SPLIT)]
             for k in (2, 1, 3):
-                send(("w_y", k), wg_v.at[plus(y, k)], wg_recv_y.at[k - 1], y_peer[k])
+                send(("g_w", k), piece, piece, z_peer[k])
 
     for k in (1, 3, 2):
         arrived(("w_y", k), wg_recv_y.at[k - 1])
@@ -229,24 +235,41 @@
     for k in (2, 1, 3):
         send(("w_z", k), wg_u.at[plus(zl, k)], wg_recv_z.at[k - 1], z_peer[k])
 
-    for kz in (0, 1, 3, 2):
-        for kx in (1, 3, 2):
+    def quarter(kz, group):
+        at_z = plus(zl, -kz)
+        rows = adj_t[pl.ds(group * N_Y, N_Y), :, pl.ds(pl.multiple_of(at_z * N_X * TILE, TILE), N_X * TILE)]
+        known = row_agg[pl.ds(at_z * N_X, N_X)].reshape(N_X * TILE, FEAT)
+        return jnp.dot(rows.reshape(N_Y * TILE, N_X * TILE), known, preferred_element_type=F32)
+
+    def arrived_quarter(kz):
+        for kx in (1, 3):
             arrived(("g_x", kz, kx), row_agg.at[col_of(x=plus(x, -kx), zl=plus(zl, -kz))])
+        if kz:
+            there = col_of(x=plus(x, 2), zl=plus(zl, -kz))
+            arrived(("g_x", kz, 2), row_agg.at[there, pl.ds(0, SPLIT)])
+            arrived(("g_w", kz), row_agg.at[there, pl.ds(SPLIT, TILE - SPLIT)])
+
+    def start(group, carry):
+        grown[group] = quarter(0, group) + quarter(1, group) + quarter(3, group)
+        return carry
+
+    def grow(kz, group, carry):
+        grown[group] += quarter(kz, group)
+        return carry
+
+    arrived_quarter(0)
+    for kz in (1, 3):
+        arrived_quarter(kz)
         if kz == 1:
             for k in (1, 3, 2):
                 arrived(("w_z", k), wg_recv_z.at[k - 1])
             wg_t[zh] = wg_u[zl] + wg_recv_z[0] + wg_recv_z[1] + wg_recv_z[2]
             send(("w_h",), wg_t.at[zh], wg_t.at[zh], high_peer)
-
-    source_b = row_agg[...].reshape(BLOCKS * TILE, FEAT)
-
-    def backward(to_c, to_h, dst):
-        for j in range(N_Y):
-            rows = adj_t[to_h * (2 * N_Y) + j * 2 + to_c]
-            dst[j] = jnp.dot(rows, source_b, preferred_element_type=F32).astype(BF16)
-
+    lax.fori_loop(0, 4, start, 0)
+    arrived_quarter(2)
     for i, (to_c, to_h) in enumerate(((1 - c, 1 - zh), (c, 1 - zh), (1 - c, zh), (c, zh))):
-        backward(to_c, to_h, part_b.at[i])
+        group = to_c * 2 + to_h
+        part_b[i] = (grown[group] + quarter(2, group)).astype(BF16).reshape(N_Y, TILE, FEAT)
         h = i // 2
         if i in (0, 2):
             send(("b_c", h), part_b.at[i], recv_c.at[h], core_peer)
@@ -255,30 +278,32 @@
             send_y[h] = (part_b[i].astype(F32) + recv_c[h].astype(F32)).astype(BF16)
             for k in (2, 1, 3):
                 send(("b_y", h, k), send_y.at[h, plus(y, k)], recv_y.at[h, k - 1], y_peer[k])
+        if i == 2:
+            for k in (1, 3, 2):
+                arrived(("w_x", k), wg_t2.at[plus(x, -k)])
+            wg_u2[zl] = ((wg_t2[0] + wg_t2[1]) + (wg_t2[2] + wg_t2[3])) * scale
+            for k in (2, 1, 3):
+                send(("w_zb", k), wg_u2.at[zl], wg_u2.at[zl], z_peer[k])
         if i == 0:
             arrived(("w_h",), wg_t.at[1 - zh])
             wg_t2[x] = wg_t[0] + wg_t[1]
             for k in (2, 1, 3):
                 send(("w_x", k), wg_t2.at[x], wg_t2.at[x], x_peer[k])
 
-    for k in (1, 3, 2):
-        arrived(("w_x", k), wg_t2.at[plus(x, -k)])
-    wg_u2[zl] = ((wg_t2[0] + wg_t2[1]) + (wg_t2[2] + wg_t2[3])) * scale
-    for k in (2, 1, 3):
-        send(("w_zb", k), wg_u2.at[zl], wg_u2.at[zl], z_peer[k])
-
-    for h in (0, 1):
+
+    def sum_y(h):
         for k in (1, 3, 2):
             arrived(("b_y", h, k), recv_y.at[h, k - 1])
-        total = send_y[h, y].astype(F32) + recv_y[h, 0].astype(F32) + recv_y[h, 1].astype(F32) + recv_y[h, 2].astype(F32)
-        if h == 0:
-            send_h[...] = total.astype(BF16)
-            send(("b_h",), send_h, recv_h, high_peer)
-            for k in (1, 3, 2):
-                arrived(("w_zb", k), wg_u2.at[plus(zl, -k)])
-            wg_v2[y] = wg_u2[...].reshape(TILE // N_Y, FEAT)
-            for k in (2, 1, 3):
-                send(("w_yb", k), wg_v2.at[y], wg_v2.at[y], y_peer[k])
+        return send_y[h, y].astype(F32) + recv_y[h, 0].astype(F32) + recv_y[h, 1].astype(F32) + recv_y[h, 2].astype(F32)
+
+    send_h[...] = sum_y(0).astype(BF16)
+    send(("b_h",), send_h, recv_h, high_peer)
+    for k in (1, 3, 2):
+        arrived(("w_zb", k), wg_u2.at[plus(zl, -k)])
+    wg_v2[y] = wg_u2[...].reshape(TILE // N_Y, FEAT)
+    for k in (2, 1, 3):
+        send(("w_yb", k), wg_v2.at[y], wg_v2.at[y], y_peer[k])
+    total = sum_y(1)
 
     for k in (1, 3, 2):
         arrived(("w_yb", k), wg_v2.at[plus(y, -k)])
@@ -354,6 +379,7 @@
             pltpu.VMEM((N_X, 8, FEAT), F32),
             pltpu.VMEM((N_ZL, 8, FEAT), F32),
             pltpu.VMEM((N_Y, TILE // N_Y, FEAT), F32),
+            pltpu.VMEM((4, N_Y * TILE, FEAT), F32),
             pltpu.SemaphoreType.DMA((10,)),
             pltpu.SemaphoreType.DMA((2,)),
             pltpu.SemaphoreType.DMA((N_COPIES,)),

time: 75.5 us -> 74.1 us (0.981)
  Pallas kernels: 74.1 us -> 72.7 us
    pallas_call x1, Pallas kernels: 72.4 us -> 71 us  [body(): pl.pallas_call(functools.partial(kernel, scale), out_shape=out_shape, in_...]
where the time goes in v3:
time: 74.1 us; the launch traced here: 74 us
  Pallas kernels  72.7 us (98%)
  between operations  1.29 us (2%)
    pallas_call x1, Pallas kernels, body(): pl.pallas_call(functools.partial(kernel, scale), out_shape=out_shape, in_...  71 us
    pallas_call x1, Pallas kernels, body(): pl.pallas_call(hand_over, out_shape=out_shape, in_specs=[pl.BlockSpec(mem...  1.71 us

profile of v3, /device:TPU:1, one launch (start us, length us, event | category | flops | bytes accessed | tf_op | source)
XLA Modules:
  0.0 74.0 jit_solution(8330999364147883054)
XLA Ops:
  1.3 71.0 %layer.1 = (bf16[128,256]{1,0:T(8,128)(2,1)}, f32[2,128,256]{2,1,0:T(8,128)}, bf16[128,256]{1,0:T(8,128)(2,1)}) custom-call(bf16[128,256]{1,0:T(8,128)(2,1)} %feat_ref.1, bf16[256,256]{1,0:T(8,128)(2,1)} %weight_hbm.1, bf16[128,256]{1,0:T(8,128)(2,1)} %cot_hbm.1, s32[1,192]{1,0:T(1,128)} %bitcast.5, s32[1,192]{1,0:T(1,128)} %bitcast.6, ...), custom_call_target="tpu_custom_call" | custom-call | tf_op jit(solution)/shard_map/layer/pallas_call | solution.py:341
  72.2 1.7 %hand_over.1 = (bf16[128,256]{1,0:T(8,128)(2,1)}, f32[2,128,256]{2,1,0:T(8,128)}, bf16[128,256]{1,0:T(8,128)(2,1)}) custom-call(bf16[128,256]{1,0:T(8,128)(2,1)} %get-tuple-element.9.out_src, f32[2,128,256]{2,1,0:T(8,128)} %get-tuple-element.10.wgrad_src, bf16[128,256]{1,0:T(8,128)(2,1)} %get-tuple-element.11.fgrad_src), custom_call_target="tpu_custom_call" | custom-call | tf_op jit(solution)/shard_map/hand_over/pallas_call | solution.py:393
